TPU v7x, 32 devices: a whole 2x2x4 slice. The times are simulated.
32 devices in a mesh: wide: 8 (over z, y), narrow: 4 (over x, core).
Axes of the slice: x: 2, y: 2, z: 4, core: 2. Of those that a mesh axis runs over, the one named last changes fastest.
Arguments:
- sources: bfloat16 [8192, 768], P('wide'), may hold values from -8 to 8
- targets: bfloat16 [65536, 768], P(('wide', 'narrow')), may hold values from -8 to 8
- pair_target: int32 [8, 12], replicated, may hold values from 0 to 63, as said below
- pair_count: int32 [8], replicated, may hold values from 8 to 12
Outputs:
- source_potential: float32 [8192], P('wide')
- target_potential: float32 [65536], P(('wide', 'narrow'))
- mapped: bfloat16 [8192, 768], P('wide')
Inputs may be any that keep to these rules, and one draw needn't show every extreme that they name: `pair_target`: source block s lies in row group w = s. Its slots k < 8 hold w * 8 + k, so every target block is paired with some source block. Its other 4 slots hold distinct target blocks of groups w - 1 and w + 1 (taken modulo the number of groups); slot 8 + m holds a block whose position within its group, divided by 2 and rounded down, equals m modulo (4).
All inputs are finite; a program needn't handle non-finite values.
Results may differ from a plain program's by a relative error of at most 0.0044.
Values may be sent and summed in bfloat16 or wider, within the bound.
A program may use at most 192 MiB of HBM per device.

v0:
```python
import math

import jax
import jax.numpy as jnp
from jax import lax
from jax.sharding import PartitionSpec as P

BLK = 1024
ITERS = 2


epsilon = 0.25
sentinel = -1e30


def passed_along(block, axis, distance):
    devices = range(lax.axis_size(axis))
    route = [((i - distance) % len(devices), i) for i in devices]
    return lax.ppermute(block, axis, route)


def combined_all(x, axis, combine):
    everything = lax.all_gather(x, axis)
    first = everything[0]

    def hop(k, so_far):
        return combine(so_far, everything[k])

    return lax.fori_loop(1, lax.axis_size(axis), hop, first)


def padded(x, sides, width):
    for axis, dim in sides:
        size, length = (lax.axis_size(axis), x.shape[dim])
        up = [(i, (i + 1) % size) for i in range(size)]
        down = [(j, i) for i, j in up]
        last = lax.slice_in_dim(x, length - width, length, axis=dim)
        first = lax.slice_in_dim(x, 0, width, axis=dim)
        before = lax.ppermute(last, axis, up)
        after = lax.ppermute(first, axis, down)
        x = jnp.concatenate([before, x, after], axis=dim)
    return x


def finish_lse(running_max, running_sum):
    present = running_sum > 0
    return jnp.where(present, running_max + jnp.log(jnp.where(present, running_sum, 1.0)), sentinel)


def send_back(partial_value, offset):
    return passed_along(partial_value, "wide", offset)


def row_potentials(partial_value):
    return combined_all(partial_value, "narrow", jnp.logaddexp)


def shards(sources, targets, pair_target, pair_count):
    feature_count = sources.shape[1]
    src_blocks = sources.shape[0] // BLK
    tgt_blocks = targets.shape[0] // BLK
    wide_count = lax.axis_size("wide")
    narrow_count = lax.axis_size("narrow")
    row_group = lax.axis_index("wide")
    column = lax.axis_index("narrow")
    group_blocks = tgt_blocks * narrow_count
    inv_root = 1.0 / math.sqrt(feature_count)
    inv_eps = 1.0 / epsilon
    log_src = -math.log(wide_count * src_blocks * BLK)
    log_tgt = -math.log(wide_count * narrow_count * tgt_blocks * BLK)
    slot_ids = jnp.arange(pair_target.shape[1], dtype=jnp.int32)
    plan_rows = lax.dynamic_slice_in_dim(pair_target, row_group * src_blocks, src_blocks, 0)
    plan_sizes = lax.dynamic_slice_in_dim(pair_count, row_group * src_blocks, src_blocks, 0)
    near_targets = padded(targets, (("wide", 0),), tgt_blocks * BLK)
    near_blocks = 3 * tgt_blocks
    local_ids = jnp.arange(near_blocks, dtype=jnp.int32)
    owner_group = (row_group + local_ids // tgt_blocks - 1 + wide_count) % wide_count
    global_ids = owner_group * group_blocks + column * tgt_blocks + local_ids % tgt_blocks
    listed = (slot_ids[None, :] < plan_sizes[:, None])[:, :, None] & (
        plan_rows[:, :, None] == global_ids[None, None, :]
    )
    linked = jnp.any(listed, axis=1).reshape(-1).astype(jnp.int32)
    unit_range = jnp.arange(src_blocks * near_blocks, dtype=jnp.int32)
    unit_source = unit_range // near_blocks
    unit_target = unit_range % near_blocks
    candidates = linked.shape[0]
    slot_total = near_targets.shape[0] // BLK
    visit_order = jnp.argsort((1 - linked) * candidates + jnp.arange(candidates, dtype=jnp.int32))
    live_count = jnp.sum(linked)

    def locate(position):
        chosen = visit_order[position]
        return (unit_source[chosen], unit_target[chosen])

    def fill_cache(position, score_cache):
        source_slab, target_slab = locate(position)
        col_block = lax.dynamic_slice_in_dim(near_targets, target_slab * BLK, BLK, 0)
        product = lax.dot_general(
            sources, col_block, (((1,), (1,)), ((), ())), preferred_element_type=jnp.float32
        )
        return lax.dynamic_update_index_in_dim(score_cache, product, position, 0)

    score_cache = lax.fori_loop(
        0, live_count, fill_cache, jnp.zeros((candidates, BLK, BLK), jnp.float32)
    )

    def slot_scores(position, potential):
        source_slab, target_slab = locate(position)
        product = lax.dynamic_index_in_dim(score_cache, position, 0, False)
        target_pot = lax.dynamic_slice_in_dim(potential, target_slab * BLK, BLK, 0)
        return (source_slab, target_slab, (target_pot[None, :] + product * inv_root) * inv_eps)

    def row_pass(potential):

        def row_visit(position, state_pair):
            running_max, running_sum = state_pair
            source_slab, target_slab, scores = slot_scores(position, potential)
            old_max = lax.dynamic_index_in_dim(running_max, source_slab, 0, False)
            old_sum = lax.dynamic_index_in_dim(running_sum, source_slab, 0, False)
            new_max = jnp.maximum(old_max, jnp.max(scores, axis=1))
            new_sum = old_sum * jnp.exp(old_max - new_max) + jnp.sum(
                jnp.exp(scores - new_max[:, None]), axis=1
            )
            return (
                lax.dynamic_update_index_in_dim(running_max, new_max, source_slab, 0),
                lax.dynamic_update_index_in_dim(running_sum, new_sum, source_slab, 0),
            )

        start = (
            jnp.full((src_blocks, BLK), sentinel, jnp.float32),
            jnp.zeros((src_blocks, BLK), jnp.float32),
        )
        running_max, running_sum = lax.fori_loop(0, live_count, row_visit, start)
        return finish_lse(running_max, running_sum).reshape(-1)

    def col_pass(source_pot):

        def col_visit(position, state_pair):
            running_max, running_sum = state_pair
            source_slab, target_slab = locate(position)
            product = lax.dynamic_index_in_dim(score_cache, position, 0, False)
            scores = (source_pot[:, None] + product * inv_root) * inv_eps
            old_max = lax.dynamic_index_in_dim(running_max, target_slab, 0, False)
            old_sum = lax.dynamic_index_in_dim(running_sum, target_slab, 0, False)
            new_max = jnp.maximum(old_max, jnp.max(scores, axis=0))
            new_sum = old_sum * jnp.exp(old_max - new_max) + jnp.sum(
                jnp.exp(scores - new_max[None, :]), axis=0
            )
            return (
                lax.dynamic_update_index_in_dim(running_max, new_max, target_slab, 0),
                lax.dynamic_update_index_in_dim(running_sum, new_sum, target_slab, 0),
            )

        start = (
            jnp.full((slot_total, BLK), sentinel, jnp.float32),
            jnp.zeros((slot_total, BLK), jnp.float32),
        )
        running_max, running_sum = lax.fori_loop(0, live_count, col_visit, start)
        return finish_lse(running_max, running_sum)

    near_pot = jnp.zeros((slot_total * BLK,), jnp.float32)
    for iteration in range(ITERS):
        row_lse = row_potentials(row_pass(near_pot))
        source_pot = epsilon * (log_src - row_lse)
        pieces = col_pass(source_pot)
        pieces = pieces.reshape(3, tgt_blocks * BLK)
        col_lse = jnp.logaddexp(
            pieces[1], jnp.logaddexp(send_back(pieces[2], 1), send_back(pieces[0], -1))
        )
        target_pot = epsilon * (log_tgt - col_lse)
        near_pot = padded(target_pot, (("wide", 0),), tgt_blocks * BLK)
    row_lse = row_potentials(row_pass(near_pot))
    source_pot = epsilon * (log_src - row_lse)

    def accumulate(position, numer):
        source_slab, target_slab, scores = slot_scores(position, near_pot)
        weights = jnp.exp(scores - row_lse[:, None]).astype(jnp.bfloat16)
        col_block = lax.dynamic_slice_in_dim(near_targets, target_slab * BLK, BLK, 0)
        partial_value = jnp.dot(weights, col_block, preferred_element_type=jnp.float32)
        return numer + partial_value

    numer = lax.fori_loop(
        0, live_count, accumulate, jnp.zeros((src_blocks * BLK, feature_count), jnp.float32)
    )
    mapped = lax.psum(numer, "narrow").astype(jnp.bfloat16)
    return (source_pot, target_pot, mapped)


def solution(mesh):
    placed = (P("wide", None), P(("wide", "narrow"), None), P(), P())
    return jax.shard_map(
        shards,
        mesh=mesh,
        in_specs=placed,
        out_specs=(P("wide"), P(("wide", "narrow")), P("wide", None)),
        check_vma=False,
    )
```

profile of v0, /device:TPU:0, one launch (start us, length us, event | category | flops | bytes accessed | tf_op | source)
XLA Modules:
  0.0 506.8 jit_solution(5354213558601483948)
XLA Ops:
  0.7 3.0 collective-permute-start
  3.7 3.1 collective-permute-start.1
  10.5 128.2 %collective-permute-done = bf16[2048,768]{1,0:T(8,128)(2,1)} collective-permute-done((bf16[2048,768]{1,0:T(8,128)(2,1)}, bf16[2048,768]{1,0:T(8,128)(2,1)}, u32[]{:S(2)}, u32[]{:S(2)}) %collective-permute-start) | collective-permute-done | bytes 3145760 | tf_op jit(solution)/shard_map/ppermute | solution.py:39
  138.8 3.8 constant_dynamic-update-slice_fusion.3
  144.6 3.7 constant_dynamic-update-slice_fusion.1
  148.3 11.5 %broadcast_in_dim.54.clone = f32[6,1024,1024]{2,1,0:T(8,128)} broadcast(f32[]{:T(128)} %constant.395.clone.1), dimensions={} | broadcast | bytes 25165828 | tf_op jit(solution)/shard_map/broadcast_in_dim | solution.py:104
  159.8 59.5 %while.130 = (s32[]{:T(128)}, f32[6,1024,1024]{2,1,0:T(8,128)}, s32[]{:T(128)}, s32[6]{0:T(128)S(1)}, s32[6]{0:T(128)S(1)}, /*index=5*/bf16[6144,768]{1,0:T(8,12...) while((s32[]{:T(128)}, f32[6,1024,1024]{2,1,0:T(8,128)}, ...), condition=%wide.region_4.5_spmd, body=%wide.region_3.4_spmd.sunk | while | flops 1610612736 | bytes 24117512 | solution.py:103
  164.2 5.2 %convolution_bitcast_fusion.2 = f32[1,1024,1024]{1,2,0:T(8,128)} fusion(bf16[1024,768]{1,0:T(8,128)(2,1)S(1)} %get-tuple-element.1382, bf16[6144,768]{1,0:T(8,128)(2,1)} %get-tuple-element.1381, s32[]{:T(128)S(6)} %select_n.376), kind=kOutput, calls=%fused_computation.clone.1 | convolution fusion | flops 1610612736 | bytes 7340036 | tf_op jit(solution)/shard_map/while/body/dot_general | solution.py:98
  169.4 5.3 %copy.53 = f32[1,1024,1024]{2,1,0:T(8,128)} copy(f32[1,1024,1024]{1,2,0:T(8,128)} %convolution_bitcast_fusion.2) | data formatting | bytes 8388608 | tf_op jit(solution)/shard_map/while/body/jit(dynamic_update_index_in_dim)/dynamic_update_slice | solution.py:101
  174.8 4.7 constant_dynamic-update-slice_fusion.5
  183.8 5.2 %convolution_bitcast_fusion.2 = f32[1,1024,1024]{1,2,0:T(8,128)} fusion(bf16[1024,768]{1,0:T(8,128)(2,1)S(1)} %get-tuple-element.1382, bf16[6144,768]{1,0:T(8,128)(2,1)} %get-tuple-element.1381, s32[]{:T(128)S(6)} %select_n.376), kind=kOutput, calls=%fused_computation.clone.1 | convolution fusion | flops 1610612736 | bytes 7340036 | tf_op jit(solution)/shard_map/while/body/dot_general | solution.py:98
  189.0 5.3 %copy.53 = f32[1,1024,1024]{2,1,0:T(8,128)} copy(f32[1,1024,1024]{1,2,0:T(8,128)} %convolution_bitcast_fusion.2) | data formatting | bytes 8388608 | tf_op jit(solution)/shard_map/while/body/jit(dynamic_update_index_in_dim)/dynamic_update_slice | solution.py:101
  194.4 4.7 constant_dynamic-update-slice_fusion.5
  203.5 5.2 %convolution_bitcast_fusion.2 = f32[1,1024,1024]{1,2,0:T(8,128)} fusion(bf16[1024,768]{1,0:T(8,128)(2,1)S(1)} %get-tuple-element.1382, bf16[6144,768]{1,0:T(8,128)(2,1)} %get-tuple-element.1381, s32[]{:T(128)S(6)} %select_n.376), kind=kOutput, calls=%fused_computation.clone.1 | convolution fusion | flops 1610612736 | bytes 7340036 | tf_op jit(solution)/shard_map/while/body/dot_general | solution.py:98
  208.7 5.3 %copy.53 = f32[1,1024,1024]{2,1,0:T(8,128)} copy(f32[1,1024,1024]{1,2,0:T(8,128)} %convolution_bitcast_fusion.2) | data formatting | bytes 8388608 | tf_op jit(solution)/shard_map/while/body/jit(dynamic_update_index_in_dim)/dynamic_update_slice | solution.py:101
  214.0 4.7 constant_dynamic-update-slice_fusion.5
  219.4 19.5 %while.131 = (s32[]{:T(128)}, f32[1,1024]{1,0:T(1,128)S(1)}, f32[1,1024]{1,0:T(1,128)S(1)}, s32[]{:T(128)}, f32[6,1024,1024]{2,1,0:T(8,128)}, /*index=5*/s32[]{:T(128)}, s32[]{:T(128)}, s32[]{:T(128)}) while((s32[]{:T(128)}, f32[1,1024]{1,0:T(1,128)S(1)}, f32[1,1024]{1,0:T(1,128)S(1)}, s32[]{:T(128)}, f32[6,1024,1024]{2,1,0:T(8,128)}, ...), condition=%wide.region_8.9_spmd, body=%wide.region_5.8_spmd.sunk | while | flops 5245957 | bytes 8437887 | solution.py:133
  222.6 3.1 fusion.72
  228.9 3.1 fusion.72
  235.2 3.1 fusion.72
  238.9 5.2 %all-gather = f32[4,1,1024]{2,1,0:T(1,128)S(1)} all-gather(f32[1,1,1024]{2,1,0:T(1,128)S(1)} %fusion.48), channel_id=1, replica_groups=mesh['wide'=8,'narrow'=4] {'narrow'}, dimensions={0}, use_global_device_ids=true | all-gather | bytes 20480 | tf_op jit(solution)/shard_map/all_gather | solution.py:23
  244.3 36.5 %while.133 = (s32[]{:T(128)}, f32[6,1024]{1,0:T(8,128)S(1)}, f32[6,1024]{1,0:T(8,128)S(1)}, s32[]{:T(128)}, s32[6]{0:T(128)S(1)}, /*index=5*/s32[6]{0:T(128)S(1)...) while((s32[]{:T(128)}, f32[6,1024]{1,0:T(8,128)S(1)}, ...), condition=%wide.region_14.15_spmd, body=%wide.region_11.14_spmd.sunk | while | flops 9439243 | bytes 8458499 | solution.py:158
  252.8 3.2 exponential_reduce_fusion.8
  264.8 3.2 exponential_reduce_fusion.8
  276.7 3.2 exponential_reduce_fusion.8
  283.4 3.1 collective-permute-start.3
  288.6 4.4 collective-permute-start.5
  294.6 32.2 %while.134 = (s32[]{:T(128)}, f32[1,1024]{1,0:T(1,128)S(1)}, f32[1,1024]{1,0:T(1,128)S(1)}, s32[]{:T(128)}, s32[6]{0:T(128)S(1)}, /*index=5*/s32[6]{0:T(128)S(1)...) while((s32[]{:T(128)}, f32[1,1024]{1,0:T(1,128)S(1)}, ...), condition=%wide.region_18.19_spmd, body=%wide.region_15.18_spmd.sunk | while | flops 9440268 | bytes 8454419 | solution.py:133
  301.9 3.3 exponential_reduce_fusion.9
  312.4 3.3 exponential_reduce_fusion.9
  322.9 3.3 exponential_reduce_fusion.9
  326.9 5.2 %all-gather.1 = f32[4,1,1024]{2,1,0:T(1,128)S(1)} all-gather(f32[1,1,1024]{2,1,0:T(1,128)S(1)} %fusion.49), channel_id=1, replica_groups=mesh['wide'=8,'narrow'=4] {'narrow'}, dimensions={0}, use_global_device_ids=true | all-gather | bytes 20480 | tf_op jit(solution)/shard_map/all_gather | solution.py:23
  332.2 36.7 %while.136 = (s32[]{:T(128)}, f32[6,1024]{1,0:T(8,128)S(1)}, f32[6,1024]{1,0:T(8,128)S(1)}, s32[]{:T(128)}, s32[6]{0:T(128)S(1)}, /*index=5*/s32[6]{0:T(128)S(1)...) while((s32[]{:T(128)}, f32[6,1024]{1,0:T(8,128)S(1)}, ...), condition=%wide.region_24.25_spmd, body=%wide.region_21.24_spmd.sunk | while | flops 9439243 | bytes 8458499 | solution.py:158
  340.9 3.2 exponential_reduce_fusion.10
  352.9 3.2 exponential_reduce_fusion.10
  364.9 3.2 exponential_reduce_fusion.10
  369.2 4.7 collective-permute-start.7
  375.6 4.8 collective-permute-start.9
  382.0 31.3 %while.137 = (s32[]{:T(128)}, f32[1,1024]{1,0:T(1,128)S(1)}, f32[1,1024]{1,0:T(1,128)S(1)}, s32[]{:T(128)}, s32[6]{0:T(128)S(1)}, /*index=5*/s32[6]{0:T(128)S(1)...) while((s32[]{:T(128)}, f32[1,1024]{1,0:T(1,128)S(1)}, ...), condition=%wide.region_28.29_spmd, body=%wide.region_25.28_spmd.sunk | while | flops 9440268 | bytes 8454419 | solution.py:133
  388.9 3.3 exponential_reduce_fusion.11
  399.2 3.3 exponential_reduce_fusion.11
  409.4 3.3 exponential_reduce_fusion.11
  413.4 5.2 %all-gather.2 = f32[4,1,1024]{2,1,0:T(1,128)S(1)} all-gather(f32[1,1,1024]{2,1,0:T(1,128)S(1)} %fusion.50), channel_id=1, replica_groups=mesh['wide'=8,'narrow'=4] {'narrow'}, dimensions={0}, use_global_device_ids=true | all-gather | bytes 20480 | tf_op jit(solution)/shard_map/all_gather | solution.py:23
  419.5 29.1 %while.139 = (s32[]{:T(128)}, f32[1024,768]{1,0:T(8,128)S(1)}, s32[]{:T(128)}, s32[6]{0:T(128)S(1)}, s32[6]{0:T(128)S(1)}, /*index=5*/f32[6144]{0:T(1024)S(1)}, ...) while((s32[]{:T(128)}, f32[1024,768]{1,0:T(8,128)S(1)}, ...), condition=%wide.region_32.33_spmd, body=%wide.region_31.32_spmd.sunk | while | flops 1616642048 | bytes 12075291 | solution.py:182
  423.9 5.1 %fusion.79 = f32[1024,768]{1,0:T(8,128)S(1)} fusion(f32[1024,768]{1,0:T(8,128)S(1)} %get-tuple-element.1625, f32[6,1024,1024]{2,1,0:T(8,128)} %get-tuple-element.1644, s32[]{:T(128)S(6)} %select_n.396, f32[1024]{0:T(1024)S(1)} %get-tuple-element.1645, f32[1024]{0:T(1024)S(1)} %dynamic_slice.263, bf16[6144,768]{1,0:T(8,128)(2,1)} %get-tuple-element.1646, ...), kind=kOutput, calls=%fused_computation.48.clone.1 | convolution fusion | flops 1616642048 | bytes 12066824 | tf_op jit(solution)/shard_map/while/body/dot_general | solution.py:179
  433.4 5.1 %fusion.79 = f32[1024,768]{1,0:T(8,128)S(1)} fusion(f32[1024,768]{1,0:T(8,128)S(1)} %get-tuple-element.1625, f32[6,1024,1024]{2,1,0:T(8,128)} %get-tuple-element.1644, s32[]{:T(128)S(6)} %select_n.396, f32[1024]{0:T(1024)S(1)} %get-tuple-element.1645, f32[1024]{0:T(1024)S(1)} %dynamic_slice.263, bf16[6144,768]{1,0:T(8,128)(2,1)} %get-tuple-element.1646, ...), kind=kOutput, calls=%fused_computation.48.clone.1 | convolution fusion | flops 1616642048 | bytes 12066824 | tf_op jit(solution)/shard_map/while/body/dot_general | solution.py:179
  442.9 5.1 %fusion.79 = f32[1024,768]{1,0:T(8,128)S(1)} fusion(f32[1024,768]{1,0:T(8,128)S(1)} %get-tuple-element.1625, f32[6,1024,1024]{2,1,0:T(8,128)} %get-tuple-element.1644, s32[]{:T(128)S(6)} %select_n.396, f32[1024]{0:T(1024)S(1)} %get-tuple-element.1645, f32[1024]{0:T(1024)S(1)} %dynamic_slice.263, bf16[6144,768]{1,0:T(8,128)(2,1)} %get-tuple-element.1646, ...), kind=kOutput, calls=%fused_computation.48.clone.1 | convolution fusion | flops 1616642048 | bytes 12066824 | tf_op jit(solution)/shard_map/while/body/dot_general | solution.py:179
  448.6 58.2 %all-reduce.1 = bf16[1024,768]{1,0:T(8,128)(2,1)} all-reduce(f32[1024,768]{1,0:T(8,128)S(1)} %get-tuple-element.674), channel_id=1, replica_groups=mesh['wide'=8,'narrow'=4] {'narrow'}, use_global_device_ids=true, to_apply=%region_33.34 | all-reduce | flops 786432 | bytes 4718592 | tf_op jit(solution)/shard_map/psum | solution.py:185
  (194 shorter events, 81.5 us)
Async XLA Ops:
  0.6 8.0 %copy-start = (s32[8,12]{1,0:T(8,128)S(1)}, s32[8,12]{1,0:T(8,128)}, u32[]{:S(2)}) copy-start(s32[8,12]{1,0:T(8,128)} %param.26) | copy-start | bytes 1156
  0.6 142.0 %copy-start.1 = (bf16[2048,768]{1,0:T(8,128)(2,1)S(1)}, bf16[2048,768]{1,0:T(8,128)(2,1)}, u32[]{:S(2)}) copy-start(bf16[2048,768]{1,0:T(8,128)(2,1)} %param.25) | copy-start | bytes 9437188
  0.7 138.1 %collective-permute-start = (bf16[2048,768]{1,0:T(8,128)(2,1)}, bf16[2048,768]{1,0:T(8,128)(2,1)}, u32[]{:S(2)}, u32[]{:S(2)}) collective-permute-start(bf16[2048,768]{1,0:T(8,128)(2,1)} %param.25), channel_id=1, source_target_pairs={{0,4},{4,8},{8,12},{12,16},{16,20},{20,24},{24,28},{28,0},{1,5},{5... | collective-permute-start | bytes 9437192 | tf_op jit(solution)/shard_map/ppermute | solution.py:39
  3.7 140.9 %collective-permute-start.1 = (bf16[2048,768]{1,0:T(8,128)(2,1)}, bf16[2048,768]{1,0:T(8,128)(2,1)}, u32[]{:S(2)}, u32[]{:S(2)}) collective-permute-start(bf16[2048,768]{1,0:T(8,128)(2,1)} %param.25), channel_id=1, source_target_pairs={{4,0},{8,4},{12,8},{16,12},{20,16},{24,20},{28,24},{0,28},{5,1},{9... | collective-permute-start | bytes 9437192 | tf_op jit(solution)/shard_map/ppermute | solution.py:40
  148.3 11.5 %copy-start.3 = (bf16[1024,768]{1,0:T(8,128)(2,1)S(1)}, bf16[1024,768]{1,0:T(8,128)(2,1)}, u32[]{:S(2)}) copy-start(bf16[1024,768]{1,0:T(8,128)(2,1)} %param.24) | copy-start | bytes 4718596
  280.9 7.2 %collective-permute-start.2 = (f32[2048]{0:T(1024)S(1)}, f32[2048]{0:T(1024)S(1)}, u32[]{:S(2)}, u32[]{:S(2)}) collective-permute-start(f32[2048]{0:T(1024)S(1)} %bitcast.271), channel_id=1, source_target_pairs={{28,0},{0,4},{4,8},{8,12},{12,16},{16,20},{20,24},{24,28},{29,1},{... | collective-permute-start | bytes 24584 | tf_op jit(solution)/shard_map/ppermute | solution.py:19
  283.4 4.7 collective-permute-start.3
  288.1 6.5 %collective-permute-start.4 = (f32[2048]{0:T(1024)S(1)}, f32[2048]{0:T(1024)S(1)}, u32[]{:S(2)}, u32[]{:S(2)}) collective-permute-start(f32[2048]{0:T(1024)S(1)} %fusion.40), channel_id=1, source_target_pairs={{0,4},{4,8},{8,12},{12,16},{16,20},{20,24},{24,28},{28,0},{1,5},{5... | collective-permute-start | bytes 24584 | tf_op jit(solution)/shard_map/ppermute | solution.py:39
  288.6 6.0 %collective-permute-start.5 = (f32[2048]{0:T(1024)S(1)}, f32[2048]{0:T(1024)S(1)}, u32[]{:S(2)}, u32[]{:S(2)}) collective-permute-start(f32[2048]{0:T(1024)S(1)} %fusion.40), channel_id=1, source_target_pairs={{4,0},{8,4},{12,8},{16,12},{20,16},{24,20},{28,24},{0,28},{5,1},{9... | collective-permute-start | bytes 24584 | tf_op jit(solution)/shard_map/ppermute | solution.py:40
  369.0 6.5 %collective-permute-start.6 = (f32[2048]{0:T(1024)S(1)}, f32[2048]{0:T(1024)S(1)}, u32[]{:S(2)}, u32[]{:S(2)}) collective-permute-start(f32[2048]{0:T(1024)S(1)} %bitcast.272), channel_id=1, source_target_pairs={{28,0},{0,4},{4,8},{8,12},{12,16},{16,20},{20,24},{24,28},{29,1},{... | collective-permute-start | bytes 24584 | tf_op jit(solution)/shard_map/ppermute | solution.py:19
  369.2 6.3 %collective-permute-start.7 = (f32[2048]{0:T(1024)S(1)}, f32[2048]{0:T(1024)S(1)}, u32[]{:S(2)}, u32[]{:S(2)}) collective-permute-start(f32[2048]{0:T(1024)S(1)} %bitcast.274), channel_id=1, source_target_pairs={{4,0},{8,4},{12,8},{16,12},{20,16},{24,20},{28,24},{0,28},{5,1},{9... | collective-permute-start | bytes 24584 | tf_op jit(solution)/shard_map/ppermute | solution.py:19
  375.5 6.5 %copy-start.2 = (f32[2048]{0:T(1024)}, f32[2048]{0:T(1024)S(1)}, u32[]{:S(2)}) copy-start(f32[2048]{0:T(1024)S(1)} %fusion.36) | copy-start | bytes 24580
  375.5 6.5 %collective-permute-start.8 = (f32[2048]{0:T(1024)S(1)}, f32[2048]{0:T(1024)S(1)}, u32[]{:S(2)}, u32[]{:S(2)}) collective-permute-start(f32[2048]{0:T(1024)S(1)} %fusion.36), channel_id=1, source_target_pairs={{0,4},{4,8},{8,12},{12,16},{16,20},{20,24},{24,28},{28,0},{1,5},{5... | collective-permute-start | bytes 24584 | tf_op jit(solution)/shard_map/ppermute | solution.py:39
  375.6 6.4 %collective-permute-start.9 = (f32[2048]{0:T(1024)S(1)}, f32[2048]{0:T(1024)S(1)}, u32[]{:S(2)}, u32[]{:S(2)}) collective-permute-start(f32[2048]{0:T(1024)S(1)} %fusion.36), channel_id=1, source_target_pairs={{4,0},{8,4},{12,8},{16,12},{20,16},{24,20},{28,24},{0,28},{5,1},{9... | collective-permute-start | bytes 24584 | tf_op jit(solution)/shard_map/ppermute | solution.py:40
where the time goes:
time: 509 us; the launch traced here: 507 us
  waiting for transfers between devices  134 us (26%)
  other arithmetic  93.6 us (18%)
  local copies, waits for them, and re-layouts  75.6 us (15%)
  blocking collectives  73.8 us (14%)
  loops' own time  70.9 us (14%)
  matrix products  31 us (6%)
  starting transfers between devices  26.5 us (5%)
    ppermute x3, waiting for transfers between devices, padded(): before = lax.ppermute(last, axis, up)  131 us
    psum x1, blocking collectives, shards(): mapped = lax.psum(numer, 'narrow').astype(jnp.bfloat16)  58.2 us
    dynamic_update_slice x6, local copies, waits for them, and re-layouts, fill_cache(): return lax.dynamic_update_index_in_dim(score_cache, product, position, 0)  30.2 us
    reduce_sum x9, other arithmetic, row_visit(): jnp.sum(jnp.exp(scores - new_max[:, None]), axis=1)  29.1 us
    another operation x2, loops' own time, col_pass(): running_max, running_sum = lax.fori_loop(0, live_count, col_visit, start)  28.5 us
    reduce_max x9, other arithmetic, row_visit(): new_max = jnp.maximum(old_max, jnp.max(scores, axis=1))  24.6 us
    another operation x3, loops' own time, row_pass(): running_max, running_sum = lax.fori_loop(0, live_count, row_visit, start)  21.8 us
    reduce_sum x6, other arithmetic, col_visit(): jnp.sum(jnp.exp(scores - new_max[None, :]), axis=0)  19.3 us
  transfers between devices with their start and end apart: 10, of which 5 were waited for; matrix products, arithmetic and copies ran while one was open for 2% of the time, Pallas kernels for 0%

commit v1 on v0

v1 whole, which is shorter than its diff:
```python
import functools
import math

import jax
import jax.numpy as jnp
from jax import lax
from jax.experimental import pallas as pl
from jax.experimental.pallas import tpu as pltpu
from jax.sharding import PartitionSpec as P

BLK = 1024
ITERS = 2
CH = 256
NCH = BLK // CH
LANES = 128
ROWS = 16
HALF = BLK // 2
PIECE = 128
NPIECE = HALF // PIECE

epsilon = 0.25
dead = -1e30
LOG2E = math.log2(math.e)
LN2 = math.log(2.0)
MESH = pl.DeviceIdType.MESH


def log2(x):
    return jnp.log(x) * LOG2E


def lse2(terms):
    top = functools.reduce(jnp.maximum, terms)
    return top, [jnp.exp2(t - top) for t in terms]


def kernel(
    wide_count, narrow_count, consts,
    plan_ref, count_ref, src_ref, tgt_ref,
    fpot_ref, gpot_ref, map_ref,
    scores, ship, landed, extra, bcast, vec, own_lse,
    row_box, col_box, far_box, bvec, part_out, part_in, cross_out, cross_in,
    ship_s, ship_r, row_s, row_r, col_s, col_r, far_s, far_r,
    part_s, part_r, cross_s, cross_r, fin_s, fin_r,
):
    scale, lsrc, ltgt, group_blocks, tgt_blocks = consts
    w = lax.axis_index("wide")
    c = lax.axis_index("narrow")

    def wide_at(d):
        return lax.rem(w + d + wide_count, wide_count)

    mates = [c + 1 - 2 * lax.rem(c, 2), c + 2 - 4 * (c // 2), 3 - c]
    wide_steps = (1, -1, 2, -2)

    barrier = pltpu.get_barrier_semaphore()
    for m in mates:
        pl.semaphore_signal(barrier, inc=1, device_id=(w, m), device_id_type=MESH)
    for d in wide_steps:
        pl.semaphore_signal(barrier, inc=1, device_id=(wide_at(d), c), device_id_type=MESH)
    pl.semaphore_wait(barrier, 7)

    slot = group_blocks + c

    def extra_of(d):
        g = wide_at(d)
        block = plan_ref[g, slot]
        live = count_ref[g] > slot
        return block, live

    my_block, my_live = extra_of(0)
    my_group = my_block // group_blocks
    from_before = my_group == wide_at(-1)
    my_pos = lax.rem(my_block, tgt_blocks)
    base = w * group_blocks + c * tgt_blocks

    def as_weight(flag, shape):
        return jnp.full(shape, jnp.where(flag, 1.0, 0.0), jnp.float32).astype(jnp.bfloat16)

    def pick(flag, a, b):
        return a * as_weight(flag, a.shape) + b * as_weight(jnp.logical_not(flag), b.shape)

    def ship_copy(k, ch):
        rows = pl.ds(pl.multiple_of(ch * CH, CH), CH)
        return pltpu.make_async_remote_copy(
            src_ref=ship.at[k, rows, :], dst_ref=landed.at[k, rows, :],
            send_sem=ship_s.at[k, ch], recv_sem=ship_r.at[k, ch],
            device_id=(wide_at(wide_steps[k]), c), device_id_type=MESH,
        )

    asked = [lax.rem(extra_of(d)[0], tgt_blocks) == 0 for d in (1, -1)]

    def ship_chunk(ch, carry):
        r0 = pl.multiple_of(ch * CH, CH)
        first = tgt_ref[pl.ds(r0, CH), :]
        second = tgt_ref[pl.ds(BLK + r0, CH), :]
        for k in range(2):
            ship[k, pl.ds(r0, CH), :] = pick(asked[k], first, second)
            ship_copy(k, ch).start()
        return carry

    lax.fori_loop(0, NCH, ship_chunk, 0)

    eye = (
        lax.broadcasted_iota(jnp.int32, (LANES, LANES), 0)
        == lax.broadcasted_iota(jnp.int32, (LANES, LANES), 1)
    )

    def dots_into(t, ch, chunk):
        cols = pl.ds(pl.multiple_of(ch * CH, CH), CH)
        scores[t, :, cols] = lax.dot_general(
            src_ref[...], chunk, (((1,), (1,)), ((), ())), preferred_element_type=jnp.float32
        ) * scale

    def own_dots(i, carry):
        r0 = pl.multiple_of(i * CH, CH)
        dots_into(i // NCH, lax.rem(i, NCH), tgt_ref[pl.ds(r0, CH), :])
        return carry

    lax.fori_loop(0, 2 * NCH, own_dots, 0)

    def row_pass(tiles, shifts):
        def step(i, carry):
            rows = pl.ds(pl.multiple_of(i * ROWS, ROWS), ROWS)
            xs = [
                scores[t, rows, :] if b is None else scores[t, rows, :] + b
                for t, b in zip(tiles, shifts)
            ]
            top = functools.reduce(jnp.maximum, xs)
            top = jnp.max(top, axis=1, keepdims=True)
            total = functools.reduce(jnp.add, [jnp.exp2(x - top) for x in xs])
            total = jnp.sum(total, axis=1, keepdims=True)
            bcast[rows, :] = jnp.broadcast_to(top + log2(total), (ROWS, LANES))
            return carry

        lax.fori_loop(0, BLK // ROWS, step, 0)
        for g in range(BLK // LANES):
            part = bcast[g * LANES:(g + 1) * LANES, :]
            vec[:, g * LANES:(g + 1) * LANES] = jnp.sum(
                jnp.where(eye, part, 0.0), axis=0, keepdims=True
            )
        return vec[...]

    def spread(v):
        for g in range(BLK // LANES):
            part = jnp.broadcast_to(v[:, g * LANES:(g + 1) * LANES], (LANES, LANES))
            col = jnp.sum(jnp.where(eye, part, 0.0), axis=1, keepdims=True)
            bcast[g * LANES:(g + 1) * LANES, :] = jnp.broadcast_to(col, (LANES, LANES))

    def col_pass(t):
        groups = BLK // LANES

        def top_step(i, tops):
            rows = pl.ds(pl.multiple_of(i * 32, 32), 32)
            a = bcast[rows, :]
            out = []
            for g in range(groups):
                x = scores[t, rows, g * LANES:(g + 1) * LANES] + a
                out.append(jnp.maximum(tops[g], jnp.max(x.reshape(4, 8, LANES), axis=0)))
            return tuple(out)

        tops = lax.fori_loop(
            0, BLK // 32, top_step,
            tuple(jnp.full((8, LANES), dead, jnp.float32) for _ in range(groups)),
        )
        tops = [jnp.max(x, axis=0, keepdims=True) for x in tops]

        def sum_step(i, sums):
            rows = pl.ds(pl.multiple_of(i * 32, 32), 32)
            a = bcast[rows, :]
            out = []
            for g in range(groups):
                x = scores[t, rows, g * LANES:(g + 1) * LANES] + a
                e = jnp.exp2(x - tops[g])
                out.append(sums[g] + jnp.sum(e.reshape(4, 8, LANES), axis=0))
            return tuple(out)

        sums = lax.fori_loop(
            0, BLK // 32, sum_step,
            tuple(jnp.zeros((8, LANES), jnp.float32) for _ in range(groups)),
        )
        return jnp.concatenate(
            [m + log2(jnp.sum(s, axis=0, keepdims=True)) for m, s in zip(tops, sums)], axis=1
        )

    def row_round(it, mine):
        row_box[it, 0] = mine
        copies = []
        for j in range(3):
            copies.append(pltpu.make_async_remote_copy(
                src_ref=row_box.at[it, 0], dst_ref=row_box.at[it, j + 1],
                send_sem=row_s.at[it, j], recv_sem=row_r.at[it, j],
                device_id=(w, mates[j]), device_id_type=MESH,
            ))
            copies[-1].start()
        for cp in copies:
            cp.wait()
        top, e = lse2([row_box[it, j] for j in range(4)])
        return top + log2((e[0] + e[1]) + (e[2] + e[3]))

    def matches(d, block):
        b, live = extra_of(d)
        return jnp.logical_and(live, b == block)

    def merge(first, others):
        terms = [first] + [jnp.where(flag, x, dead) for flag, x in others]
        top, e = lse2(terms)
        return top + log2(functools.reduce(jnp.add, e))

    def col_round(it):
        for t in range(3):
            col_box[it, 0, t] = col_pass(t)
        copies = []
        for k in range(2):
            copies.append(pltpu.make_async_remote_copy(
                src_ref=col_box.at[it, 0], dst_ref=col_box.at[it, k + 1],
                send_sem=col_s.at[it, k], recv_sem=col_r.at[it, k],
                device_id=(wide_at(wide_steps[k]), c), device_id_type=MESH,
            ))
        for k in range(2):
            copies.append(pltpu.make_async_remote_copy(
                src_ref=col_box.at[it, 0, 2], dst_ref=far_box.at[it, k],
                send_sem=far_s.at[it, k], recv_sem=far_r.at[it, k],
                device_id=(wide_at(wide_steps[k + 2]), c), device_id_type=MESH,
            ))
        for cp in copies:
            cp.start()
        for cp in copies:
            cp.wait()
        before, after = col_box[it, 1, 2], col_box[it, 2, 2]
        for b in range(2):
            total = merge(
                col_box[it, 0, b],
                [(matches(-1, base + b), before), (matches(1, base + b), after)],
            )
            bvec[b] = ltgt - total
        owner = jnp.where(
            from_before,
            jnp.where(my_pos == 0, col_box[it, 1, 0], col_box[it, 1, 1]),
            jnp.where(my_pos == 0, col_box[it, 2, 0], col_box[it, 2, 1]),
        )
        third_flag = jnp.where(
            from_before,
            jnp.where(matches(-2, my_block), 1, 0),
            jnp.where(matches(2, my_block), 1, 0),
        ) == 1
        third = jnp.where(from_before, far_box[it, 0], far_box[it, 1])
        total = merge(owner, [(my_live, col_box[it, 0, 2]), (third_flag, third)])
        bvec[2] = jnp.where(my_live, ltgt - total, dead)

    own_lse[...] = row_pass([0, 1], [None, None])

    def land(ch, carry):
        rows = pl.ds(pl.multiple_of(ch * CH, CH), CH)
        for k in range(2):
            ship_copy(k, ch).wait()
        chunk = pick(from_before, landed[0, rows, :], landed[1, rows, :])
        extra[rows, :] = chunk
        dots_into(2, ch, chunk)
        return carry

    lax.fori_loop(0, NCH, land, 0)

    extra_lse = jnp.where(my_live, row_pass([2], [None]), dead)
    top, e = lse2([own_lse[...], extra_lse])
    total = row_round(0, top + log2(e[0] + e[1]))
    for it in range(ITERS):
        spread(lsrc - total)
        col_round(it)
        total = row_round(it + 1, row_pass([0, 1, 2], [bvec[0], bvec[1], bvec[2]]))
    fpot_ref[...] = (epsilon * LN2) * (lsrc - total)
    for b in range(2):
        gpot_ref[b] = (epsilon * LN2) * bvec[b]
    spread(total)

    def bary(r0):
        rows = pl.ds(pl.multiple_of(r0, PIECE), PIECE)
        level = bcast[rows, :]
        level = jnp.concatenate([level] * (BLK // LANES), axis=1)
        numer = None
        for t in range(3):
            weights = jnp.exp2(scores[t, rows, :] + bvec[t] - level).astype(jnp.bfloat16)
            block = extra[...] if t == 2 else tgt_ref[t * BLK:(t + 1) * BLK, :]
            term = jnp.dot(weights, block, preferred_element_type=jnp.float32)
            numer = term if numer is None else numer + term
        return numer

    side = lax.rem(c, 2)
    mine0 = side * HALF
    theirs0 = HALF - mine0

    def piece_rows(p):
        return pl.ds(pl.multiple_of(p * PIECE, PIECE), PIECE)

    def part_copy(p):
        return pltpu.make_async_remote_copy(
            src_ref=part_out.at[piece_rows(p), :], dst_ref=part_in.at[piece_rows(p), :],
            send_sem=part_s.at[p], recv_sem=part_r.at[p],
            device_id=(w, mates[0]), device_id_type=MESH,
        )

    def cross_copy(p):
        return pltpu.make_async_remote_copy(
            src_ref=cross_out.at[piece_rows(p), :], dst_ref=cross_in.at[piece_rows(p), :],
            send_sem=cross_s.at[p], recv_sem=cross_r.at[p],
            device_id=(w, mates[1]), device_id_type=MESH,
        )

    def final_copy(p):
        rows = pl.ds(pl.multiple_of(mine0 + p * PIECE, PIECE), PIECE)
        return pltpu.make_async_remote_copy(
            src_ref=map_ref.at[rows, :], dst_ref=map_ref.at[rows, :],
            send_sem=fin_s.at[p], recv_sem=fin_r.at[p],
            device_id=(w, mates[0]), device_id_type=MESH,
        )

    def send_part(p, carry):
        part_out[piece_rows(p), :] = bary(theirs0 + p * PIECE).astype(jnp.bfloat16)
        part_copy(p).start()
        mine = bary(mine0 + p * PIECE)
        part_copy(p).wait()
        mine = mine + part_in[piece_rows(p), :].astype(jnp.float32)
        cross_out[piece_rows(p), :] = mine.astype(jnp.bfloat16)
        cross_copy(p).start()
        return carry

    lax.fori_loop(0, NPIECE, send_part, 0)

    def finish(p, carry):
        cross_copy(p).wait()
        both = cross_out[piece_rows(p), :].astype(jnp.float32) + cross_in[
            piece_rows(p), :
        ].astype(jnp.float32)
        rows = pl.ds(pl.multiple_of(mine0 + p * PIECE, PIECE), PIECE)
        map_ref[rows, :] = both.astype(jnp.bfloat16)
        final_copy(p).start()
        return carry

    lax.fori_loop(0, NPIECE, finish, 0)

    def drain(p, carry):
        final_copy(p).wait()
        return carry

    lax.fori_loop(0, NPIECE, drain, 0)


def shards(sources, targets, pair_target, pair_count):
    features = sources.shape[1]
    src_blocks = sources.shape[0] // BLK
    tgt_blocks = targets.shape[0] // BLK
    wide_count = lax.axis_size("wide")
    narrow_count = lax.axis_size("narrow")
    group_blocks = tgt_blocks * narrow_count
    assert src_blocks == 1 and tgt_blocks == 2 and narrow_count == 4
    assert pair_target.shape[1] == group_blocks + narrow_count and wide_count >= 5
    scale = LOG2E / (math.sqrt(features) * epsilon)
    lsrc = -math.log2(wide_count * src_blocks * BLK)
    ltgt = -math.log2(wide_count * narrow_count * tgt_blocks * BLK)
    consts = (scale, lsrc, ltgt, group_blocks, tgt_blocks)
    vm = pl.BlockSpec(memory_space=pltpu.VMEM)
    sm = pl.BlockSpec(memory_space=pltpu.SMEM)
    f32, bf16 = jnp.float32, jnp.bfloat16
    rounds = ITERS + 1
    dma = pltpu.SemaphoreType.DMA
    fpot, gpot, mapped = pl.pallas_call(
        functools.partial(kernel, wide_count, narrow_count, consts),
        out_shape=(
            jax.ShapeDtypeStruct((1, BLK), f32),
            jax.ShapeDtypeStruct((tgt_blocks, 1, BLK), f32),
            jax.ShapeDtypeStruct((BLK, features), bf16),
        ),
        in_specs=[sm, sm, vm, vm],
        out_specs=(vm, vm, vm),
        scratch_shapes=[
            pltpu.VMEM((3, BLK, BLK), f32),
            pltpu.VMEM((2, BLK, features), bf16),
            pltpu.VMEM((2, BLK, features), bf16),
            pltpu.VMEM((BLK, features), bf16),
            pltpu.VMEM((BLK, LANES), f32),
            pltpu.VMEM((1, BLK), f32),
            pltpu.VMEM((1, BLK), f32),
            pltpu.VMEM((rounds, 4, 1, BLK), f32),
            pltpu.VMEM((ITERS, 3, 3, 1, BLK), f32),
            pltpu.VMEM((ITERS, 2, 1, BLK), f32),
            pltpu.VMEM((3, 1, BLK), f32),
            pltpu.VMEM((HALF, features), bf16),
            pltpu.VMEM((HALF, features), bf16),
            pltpu.VMEM((HALF, features), bf16),
            pltpu.VMEM((HALF, features), bf16),
            dma((2, NCH)), dma((2, NCH)),
            dma((rounds, 3)), dma((rounds, 3)),
            dma((ITERS, 2)), dma((ITERS, 2)),
            dma((ITERS, 2)), dma((ITERS, 2)),
            dma((NPIECE,)), dma((NPIECE,)),
            dma((NPIECE,)), dma((NPIECE,)),
            dma((NPIECE,)), dma((NPIECE,)),
        ],
        compiler_params=pltpu.CompilerParams(
            collective_id=0, has_side_effects=True, vmem_limit_bytes=48 * 1024 * 1024
        ),
        cost_estimate=pl.CostEstimate(
            flops=12 * BLK * BLK * features, bytes_accessed=8 * BLK * features,
            transcendentals=18 * BLK * BLK,
        ),
    )(pair_target, pair_count, sources, targets)
    return (fpot.reshape(-1), gpot.reshape(-1), mapped)


def solution(mesh):
    placed = (P("wide", None), P(("wide", "narrow"), None), P(), P())
    return jax.shard_map(
        shards,
        mesh=mesh,
        in_specs=placed,
        out_specs=(P("wide"), P(("wide", "narrow")), P("wide", None)),
        check_vma=False,
    )
```

time: 509 us -> 171 us (0.34)
  Pallas kernels: 0 us -> 165 us
  waiting for transfers between devices: 134 us -> 0 us
  other arithmetic: 93.6 us -> 0 us
  blocking collectives: 73.8 us -> 0 us
  loops' own time: 70.9 us -> 0 us
  local copies, waits for them, and re-layouts: 75.6 us -> 5.08 us
  matrix products: 31 us -> 0 us
  starting transfers between devices: 26.5 us -> 0 us
    pallas_call x0 -> x1, Pallas kernels: none -> 165 us  [shards(): pl.pallas_call(functools.partial(kernel, wide_count, narrow_count, consts...]
    ppermute x10 -> x0, waiting for transfers between devices: 134 us -> none  [the longest x3 131 us: padded(): before = lax.ppermute(last, axis, up)]
    another operation x10 -> x0, loops' own time: 70.9 us -> none  [the longest x2 28.5 us: col_pass(): running_max, running_sum = lax.fori_loop(0, live_count, col_visit, start)]
    psum x1 -> x0, blocking collectives: 58.2 us -> none  [shards(): mapped = lax.psum(numer, 'narrow').astype(jnp.bfloat16)]
    reduce_sum x15 -> x0, other arithmetic: 48.4 us -> none  [the longest x9 29.1 us: row_visit(): jnp.sum(jnp.exp(scores - new_max[:, None]), axis=1)]
    reduce_max x15 -> x0, other arithmetic: 41.4 us -> none  [the longest x9 24.6 us: row_visit(): new_max = jnp.maximum(old_max, jnp.max(scores, axis=1))]
    dynamic_update_slice x18 -> x0, local copies, waits for them, and re-layouts: 31.5 us -> none  [the longest x6 30.2 us: fill_cache(): return lax.dynamic_update_index_in_dim(score_cache, product, position, 0)]
    dot_general x6 -> x0, matrix products: 31 us -> none  [the longest x3 15.7 us: fill_cache(): lax.dot_general(sources, col_block, (((1,), (1,)), ((), ())), preferred_e...]
  transfers between devices with their start and end apart: 10 -> 0, of which waited for: 5 -> 0; matrix products, arithmetic and copies ran while one was open for 2% -> 0% of each run, Pallas kernels for 0% -> 0%
where the time goes in v1:
time: 171 us
  Pallas kernels  165 us (96%)
  local copies, waits for them, and re-layouts  5.08 us (3%)
    pallas_call x1, Pallas kernels, shards(): pl.pallas_call(functools.partial(kernel, wide_count, narrow_count, consts...  165 us
    unnamed x9, local copies, waits for them, and re-layouts  5.08 us

profile of v1, /device:TPU:0, one launch (start us, length us, event | category | flops | bytes accessed | tf_op | source)
XLA Modules:
  0.0 170.5 jit_solution(15361907405891448074)
XLA Ops:
  0.6 0.0 copy-start
  0.6 1.4 copy-done
  2.0 0.0 copy-start.1
  2.0 0.7 copy-done.1
  2.7 0.0 copy-start.2
  2.7 0.7 copy-done.2
  3.4 164.8 %shard_map.67 = (f32[1,1024]{1,0:T(1,128)S(1)}, f32[2,1,1024]{2,1,0:T(1,128)S(1)}, bf16[1024,768]{1,0:T(8,128)(2,1)S(1)}) custom-call(s32[8,12]{1,0:T(8,128)S(1)} %copy-done.1, s32[8]{0:T(128)S(1)} %copy-done.2, bf16[1024,768]{1,0:T(8,128)(2,1)S(1)} %copy-done, bf16[2048,768]{1,0:T(8,128)(2,1)} %tgt_ref.1), custom_call_target="tpu_custom_call" | custom-call | flops 9663676416 | bytes 6291456 | tf_op jit(solution)/shard_map/pallas_call | solution.py:366
  168.2 0.6 copy.10
  168.8 0.6 copy.11
  169.4 1.1 copy.12
Async XLA Ops:
  0.6 1.4 copy-start
  2.0 0.7 copy-start.1
  2.7 0.7 copy-start.2

commit v2 on v1

--- a/solution.py
+++ b/solution.py
@@ -12,10 +12,13 @@
 ITERS = 2
 CH = 256
 NCH = BLK // CH
+SHIP = 128
+NSHIP = BLK // SHIP
 LANES = 128
 ROWS = 16
+STRIP = 64
 HALF = BLK // 2
-PIECE = 128
+PIECE = 256
 NPIECE = HALF // PIECE
 
 epsilon = 0.25
@@ -34,13 +37,20 @@
     return top, [jnp.exp2(t - top) for t in terms]
 
 
+def tree(op, terms):
+    while len(terms) > 1:
+        pairs = [op(a, b) for a, b in zip(terms[::2], terms[1::2])]
+        terms = pairs + terms[len(terms) - len(terms) % 2:]
+    return terms[0]
+
+
 def kernel(
     wide_count, narrow_count, consts,
     plan_ref, count_ref, src_ref, tgt_ref,
     fpot_ref, gpot_ref, map_ref,
-    scores, ship, landed, extra, bcast, vec, own_lse,
+    scores, relay_out, relay_in, ship, extra, bcast, lane_top, lane_sum, vec, own_lse,
     row_box, col_box, far_box, bvec, part_out, part_in, cross_out, cross_in,
-    ship_s, ship_r, row_s, row_r, col_s, col_r, far_s, far_r,
+    relay_s, relay_r, ship_s, ship_r, row_s, row_r, col_s, col_r, far_s, far_r,
     part_s, part_r, cross_s, cross_r, fin_s, fin_r,
 ):
     scale, lsrc, ltgt, group_blocks, tgt_blocks = consts
@@ -80,26 +90,43 @@
     def pick(flag, a, b):
         return a * as_weight(flag, a.shape) + b * as_weight(jnp.logical_not(flag), b.shape)
 
-    def ship_copy(k, ch):
-        rows = pl.ds(pl.multiple_of(ch * CH, CH), CH)
+    even = lax.rem(w, 2) == 0
+    away = jnp.where(even, wide_at(-2), wide_at(2))
+    partner = jnp.where(even, w + 1, w - 1)
+    user = jnp.where(even, wide_at(-1), wide_at(1))
+
+    def chunk_rows(ch):
+        return pl.ds(pl.multiple_of(ch * SHIP, SHIP), SHIP)
+
+    def relay_copy(ch):
         return pltpu.make_async_remote_copy(
-            src_ref=ship.at[k, rows, :], dst_ref=landed.at[k, rows, :],
-            send_sem=ship_s.at[k, ch], recv_sem=ship_r.at[k, ch],
-            device_id=(wide_at(wide_steps[k]), c), device_id_type=MESH,
-        )
-
-    asked = [lax.rem(extra_of(d)[0], tgt_blocks) == 0 for d in (1, -1)]
-
-    def ship_chunk(ch, carry):
-        r0 = pl.multiple_of(ch * CH, CH)
-        first = tgt_ref[pl.ds(r0, CH), :]
-        second = tgt_ref[pl.ds(BLK + r0, CH), :]
-        for k in range(2):
-            ship[k, pl.ds(r0, CH), :] = pick(asked[k], first, second)
-            ship_copy(k, ch).start()
+            src_ref=relay_out.at[chunk_rows(ch), :], dst_ref=relay_in.at[chunk_rows(ch), :],
+            send_sem=relay_s.at[ch], recv_sem=relay_r.at[ch],
+            device_id=(away, c), device_id_type=MESH,
+        )
+
+    def ship_copy(ch):
+        return pltpu.make_async_remote_copy(
+            src_ref=ship.at[chunk_rows(ch), :], dst_ref=extra.at[chunk_rows(ch), :],
+            send_sem=ship_s.at[ch], recv_sem=ship_r.at[ch],
+            device_id=(partner, c), device_id_type=MESH,
+        )
+
+    def own_chunk(first_wanted, ch):
+        r0 = pl.multiple_of(ch * SHIP, SHIP)
+        return pick(first_wanted, tgt_ref[pl.ds(r0, SHIP), :], tgt_ref[pl.ds(BLK + r0, SHIP), :])
+
+    user_first = lax.rem(plan_ref[user, slot], tgt_blocks) == 0
+    partner_block = plan_ref[partner, slot]
+    partner_first = lax.rem(partner_block, tgt_blocks) == 0
+    partner_mine = partner_block // group_blocks == w
+
+    def relay_chunk(ch, carry):
+        relay_out[chunk_rows(ch), :] = own_chunk(user_first, ch)
+        relay_copy(ch).start()
         return carry
 
-    lax.fori_loop(0, NCH, ship_chunk, 0)
+    lax.fori_loop(0, NSHIP, relay_chunk, 0)
 
     eye = (
         lax.broadcasted_iota(jnp.int32, (LANES, LANES), 0)
@@ -112,30 +139,52 @@
             src_ref[...], chunk, (((1,), (1,)), ((), ())), preferred_element_type=jnp.float32
         ) * scale
 
-    def own_dots(i, carry):
+    def own_dots(i):
         r0 = pl.multiple_of(i * CH, CH)
         dots_into(i // NCH, lax.rem(i, NCH), tgt_ref[pl.ds(r0, CH), :])
+
+    def land(i):
+        ship_copy(2 * i).wait()
+        ship_copy(2 * i + 1).wait()
+        dots_into(2, i, extra[pl.ds(pl.multiple_of(i * CH, CH), CH), :])
+
+    def forward(ch, carry):
+        own_dots(ch)
+        relay_copy(ch).wait()
+        ship[chunk_rows(ch), :] = pick(
+            partner_mine, own_chunk(partner_first, ch), relay_in[chunk_rows(ch), :]
+        )
+        ship_copy(ch).start()
+
+        @pl.when(jnp.logical_and(lax.rem(ch, 2) == 1, ch >= 3))
+        def _():
+            land((ch - 3) // 2)
+
         return carry
 
-    lax.fori_loop(0, 2 * NCH, own_dots, 0)
+    lax.fori_loop(0, NSHIP, forward, 0)
 
     def row_pass(tiles, shifts):
         def step(i, carry):
-            rows = pl.ds(pl.multiple_of(i * ROWS, ROWS), ROWS)
-            xs = [
-                scores[t, rows, :] if b is None else scores[t, rows, :] + b
-                for t, b in zip(tiles, shifts)
-            ]
-            top = functools.reduce(jnp.maximum, xs)
-            top = jnp.max(top, axis=1, keepdims=True)
-            total = functools.reduce(jnp.add, [jnp.exp2(x - top) for x in xs])
-            total = jnp.sum(total, axis=1, keepdims=True)
-            bcast[rows, :] = jnp.broadcast_to(top + log2(total), (ROWS, LANES))
+            for h in range(2):
+                rows = pl.ds(pl.multiple_of((2 * i + h) * ROWS, ROWS), ROWS)
+                xs = []
+                for t, b in zip(tiles, shifts):
+                    for g in range(BLK // LANES):
+                        x = scores[t, rows, g * LANES:(g + 1) * LANES]
+                        xs.append(x if b is None else x + b[:, g * LANES:(g + 1) * LANES])
+                top = tree(jnp.maximum, xs)
+                lane_top[rows, :] = top
+                lane_sum[rows, :] = tree(jnp.add, [jnp.exp2(x - top) for x in xs])
             return carry
 
-        lax.fori_loop(0, BLK // ROWS, step, 0)
+        lax.fori_loop(0, BLK // (2 * ROWS), step, 0)
         for g in range(BLK // LANES):
-            part = bcast[g * LANES:(g + 1) * LANES, :]
+            rows = slice(g * LANES, (g + 1) * LANES)
+            tops = lane_top[rows, :]
+            top = jnp.max(tops, axis=1, keepdims=True)
+            total = jnp.sum(lane_sum[rows, :] * jnp.exp2(tops - top), axis=1, keepdims=True)
+            part = jnp.broadcast_to(top + log2(total), (LANES, LANES))
             vec[:, g * LANES:(g + 1) * LANES] = jnp.sum(
                 jnp.where(eye, part, 0.0), axis=0, keepdims=True
             )
@@ -151,32 +200,32 @@
         groups = BLK // LANES
 
         def top_step(i, tops):
-            rows = pl.ds(pl.multiple_of(i * 32, 32), 32)
+            rows = pl.ds(pl.multiple_of(i * STRIP, STRIP), STRIP)
             a = bcast[rows, :]
             out = []
             for g in range(groups):
                 x = scores[t, rows, g * LANES:(g + 1) * LANES] + a
-                out.append(jnp.maximum(tops[g], jnp.max(x.reshape(4, 8, LANES), axis=0)))
+                out.append(jnp.maximum(tops[g], jnp.max(x.reshape(STRIP // 8, 8, LANES), axis=0)))
             return tuple(out)
 
         tops = lax.fori_loop(
-            0, BLK // 32, top_step,
+            0, BLK // STRIP, top_step,
             tuple(jnp.full((8, LANES), dead, jnp.float32) for _ in range(groups)),
         )
         tops = [jnp.max(x, axis=0, keepdims=True) for x in tops]
 
         def sum_step(i, sums):
-            rows = pl.ds(pl.multiple_of(i * 32, 32), 32)
+            rows = pl.ds(pl.multiple_of(i * STRIP, STRIP), STRIP)
             a = bcast[rows, :]
             out = []
             for g in range(groups):
                 x = scores[t, rows, g * LANES:(g + 1) * LANES] + a
                 e = jnp.exp2(x - tops[g])
-                out.append(sums[g] + jnp.sum(e.reshape(4, 8, LANES), axis=0))
+                out.append(sums[g] + jnp.sum(e.reshape(STRIP // 8, 8, LANES), axis=0))
             return tuple(out)
 
         sums = lax.fori_loop(
-            0, BLK // 32, sum_step,
+            0, BLK // STRIP, sum_step,
             tuple(jnp.zeros((8, LANES), jnp.float32) for _ in range(groups)),
         )
         return jnp.concatenate(
@@ -250,16 +299,7 @@
 
     own_lse[...] = row_pass([0, 1], [None, None])
 
-    def land(ch, carry):
-        rows = pl.ds(pl.multiple_of(ch * CH, CH), CH)
-        for k in range(2):
-            ship_copy(k, ch).wait()
-        chunk = pick(from_before, landed[0, rows, :], landed[1, rows, :])
-        extra[rows, :] = chunk
-        dots_into(2, ch, chunk)
-        return carry
-
-    lax.fori_loop(0, NCH, land, 0)
+    land(NCH - 1)
 
     extra_lse = jnp.where(my_live, row_pass([2], [None]), dead)
     top, e = lse2([own_lse[...], extra_lse])
@@ -353,7 +393,7 @@
     narrow_count = lax.axis_size("narrow")
     group_blocks = tgt_blocks * narrow_count
     assert src_blocks == 1 and tgt_blocks == 2 and narrow_count == 4
-    assert pair_target.shape[1] == group_blocks + narrow_count and wide_count >= 5
+    assert pair_target.shape[1] == group_blocks + narrow_count and wide_count >= 5 and wide_count % 2 == 0
     scale = LOG2E / (math.sqrt(features) * epsilon)
     lsrc = -math.log2(wide_count * src_blocks * BLK)
     ltgt = -math.log2(wide_count * narrow_count * tgt_blocks * BLK)
@@ -374,9 +414,12 @@
         out_specs=(vm, vm, vm),
         scratch_shapes=[
             pltpu.VMEM((3, BLK, BLK), f32),
-            pltpu.VMEM((2, BLK, features), bf16),
-            pltpu.VMEM((2, BLK, features), bf16),
             pltpu.VMEM((BLK, features), bf16),
+            pltpu.VMEM((BLK, features), bf16),
+            pltpu.VMEM((BLK, features), bf16),
+            pltpu.VMEM((BLK, features), bf16),
+            pltpu.VMEM((BLK, LANES), f32),
+            pltpu.VMEM((BLK, LANES), f32),
             pltpu.VMEM((BLK, LANES), f32),
             pltpu.VMEM((1, BLK), f32),
             pltpu.VMEM((1, BLK), f32),
@@ -388,7 +431,8 @@
             pltpu.VMEM((HALF, features), bf16),
             pltpu.VMEM((HALF, features), bf16),
             pltpu.VMEM((HALF, features), bf16),
-            dma((2, NCH)), dma((2, NCH)),
+            dma((NSHIP,)), dma((NSHIP,)),
+            dma((NSHIP,)), dma((NSHIP,)),
             dma((rounds, 3)), dma((rounds, 3)),
             dma((ITERS, 2)), dma((ITERS, 2)),
             dma((ITERS, 2)), dma((ITERS, 2)),

time: 171 us -> 115 us (0.67)
  Pallas kernels: 165 us -> 109 us
    pallas_call x1, Pallas kernels: 165 us -> 109 us  [shards(): pl.pallas_call(functools.partial(kernel, wide_count, narrow_count, consts...]
where the time goes in v2:
time: 115 us; the launch traced here: 114 us
  Pallas kernels  109 us (95%)
  local copies, waits for them, and re-layouts  5.08 us (4%)
    pallas_call x1, Pallas kernels, shards(): pl.pallas_call(functools.partial(kernel, wide_count, narrow_count, consts...  109 us
    unnamed x9, local copies, waits for them, and re-layouts  5.08 us

profile of v2, /device:TPU:0, one launch (start us, length us, event | category | flops | bytes accessed | tf_op | source)
XLA Modules:
  0.0 114.4 jit_solution(6387900004195219191)
XLA Ops:
  0.6 0.0 copy-start
  0.6 1.4 %copy-done = bf16[1024,768]{1,0:T(8,128)(2,1)S(1)} copy-done((bf16[1024,768]{1,0:T(8,128)(2,1)S(1)}, bf16[1024,768]{1,0:T(8,128)(2,1)}, u32[]{:S(2)}) %copy-start) | copy-done | bytes 1572888
  2.0 0.0 copy-start.1
  2.0 0.7 copy-done.1
  2.7 0.0 copy-start.2
  2.7 0.7 copy-done.2
  3.4 108.7 %shard_map.67 = (f32[1,1024]{1,0:T(1,128)S(1)}, f32[2,1,1024]{2,1,0:T(1,128)S(1)}, bf16[1024,768]{1,0:T(8,128)(2,1)S(1)}) custom-call(s32[8,12]{1,0:T(8,128)S(1)} %copy-done.1, s32[8]{0:T(128)S(1)} %copy-done.2, bf16[1024,768]{1,0:T(8,128)(2,1)S(1)} %copy-done, bf16[2048,768]{1,0:T(8,128)(2,1)} %tgt_ref.1), custom_call_target="tpu_custom_call" | custom-call | flops 9663676416 | bytes 6291456 | tf_op jit(solution)/shard_map/pallas_call | solution.py:406
  112.0 0.6 copy.10
  112.6 0.6 copy.11
  113.2 1.1 copy.12
Async XLA Ops:
  0.6 1.4 %copy-start = (bf16[1024,768]{1,0:T(8,128)(2,1)S(1)}, bf16[1024,768]{1,0:T(8,128)(2,1)}, u32[]{:S(2)}) copy-start(bf16[1024,768]{1,0:T(8,128)(2,1)} %src_ref.1) | copy-start | bytes 4718596
  2.0 0.7 copy-start.1
  2.7 0.7 copy-start.2

commit v3 on v2

--- a/solution.py
+++ b/solution.py
@@ -12,13 +12,14 @@
 ITERS = 2
 CH = 256
 NCH = BLK // CH
-SHIP = 128
+SHIP = 64
 NSHIP = BLK // SHIP
+PARTS = CH // SHIP
 LANES = 128
 ROWS = 16
 STRIP = 64
 HALF = BLK // 2
-PIECE = 256
+PIECE = 128
 NPIECE = HALF // PIECE
 
 epsilon = 0.25
@@ -46,12 +47,12 @@
 
 def kernel(
     wide_count, narrow_count, consts,
-    plan_ref, count_ref, src_ref, tgt_ref,
+    plan_ref, count_ref, src_hbm, tgt_hbm,
     fpot_ref, gpot_ref, map_ref,
-    scores, relay_out, relay_in, ship, extra, bcast, lane_top, lane_sum, vec, own_lse,
+    src_ref, tgt_ref, scores, relay_out, relay_in, ship, extra, bcast, lane_top, lane_sum, vec, qvec, own_lse,
     row_box, col_box, far_box, bvec, part_out, part_in, cross_out, cross_in,
     relay_s, relay_r, ship_s, ship_r, row_s, row_r, col_s, col_r, far_s, far_r,
-    part_s, part_r, cross_s, cross_r, fin_s, fin_r,
+    part_s, part_r, cross_s, cross_r, fin_s, fin_r, load_sem,
 ):
     scale, lsrc, ltgt, group_blocks, tgt_blocks = consts
     w = lax.axis_index("wide")
@@ -62,6 +63,11 @@
 
     mates = [c + 1 - 2 * lax.rem(c, 2), c + 2 - 4 * (c // 2), 3 - c]
     wide_steps = (1, -1, 2, -2)
+
+    load_tgt = pltpu.make_async_copy(tgt_hbm, tgt_ref, load_sem.at[0])
+    load_src = pltpu.make_async_copy(src_hbm, src_ref, load_sem.at[1])
+    load_tgt.start()
+    load_src.start()
 
     barrier = pltpu.get_barrier_semaphore()
     for m in mates:
@@ -69,6 +75,7 @@
     for d in wide_steps:
         pl.semaphore_signal(barrier, inc=1, device_id=(wide_at(d), c), device_id_type=MESH)
     pl.semaphore_wait(barrier, 7)
+    load_tgt.wait()
 
     slot = group_blocks + c
 
@@ -144,21 +151,26 @@
         dots_into(i // NCH, lax.rem(i, NCH), tgt_ref[pl.ds(r0, CH), :])
 
     def land(i):
-        ship_copy(2 * i).wait()
-        ship_copy(2 * i + 1).wait()
+        for p in range(PARTS):
+            ship_copy(PARTS * i + p).wait()
         dots_into(2, i, extra[pl.ds(pl.multiple_of(i * CH, CH), CH), :])
 
+    load_src.wait()
+
     def forward(ch, carry):
-        own_dots(ch)
+        @pl.when(lax.rem(ch, 2) == 0)
+        def _():
+            own_dots(ch // 2)
+
         relay_copy(ch).wait()
         ship[chunk_rows(ch), :] = pick(
             partner_mine, own_chunk(partner_first, ch), relay_in[chunk_rows(ch), :]
         )
         ship_copy(ch).start()
 
-        @pl.when(jnp.logical_and(lax.rem(ch, 2) == 1, ch >= 3))
+        @pl.when(jnp.logical_and(lax.rem(ch, PARTS) == 1, ch > PARTS))
         def _():
-            land((ch - 3) // 2)
+            land((ch - PARTS) // PARTS)
 
         return carry
 
@@ -190,6 +202,66 @@
             )
         return vec[...]
 
+    def to_row():
+        for g in range(BLK // LANES):
+            col = jnp.sum(lane_sum[g * LANES:(g + 1) * LANES, :], axis=1, keepdims=True)
+            part = jnp.broadcast_to(col, (LANES, LANES))
+            vec[:, g * LANES:(g + 1) * LANES] = jnp.sum(
+                jnp.where(eye, part, 0.0), axis=0, keepdims=True
+            )
+        return vec[...]
+
+    def plan_pass():
+        def step(i, carry):
+            for h in range(2):
+                rows = pl.ds(pl.multiple_of((2 * i + h) * ROWS, ROWS), ROWS)
+                a = bcast[rows, :]
+                es = []
+                for t in range(3):
+                    for g in range(BLK // LANES):
+                        cols = slice(g * LANES, (g + 1) * LANES)
+                        e = jnp.exp2(scores[t, rows, cols] + a + (bvec[t, :, cols] - ltgt))
+                        scores[t, rows, cols] = e
+                        es.append(e)
+                lane_sum[rows, :] = tree(jnp.add, es)
+            return carry
+
+        lax.fori_loop(0, BLK // (2 * ROWS), step, 0)
+        return to_row()
+
+    def scaled_row_sums():
+        def step(i, carry):
+            for h in range(2):
+                rows = pl.ds(pl.multiple_of((2 * i + h) * ROWS, ROWS), ROWS)
+                es = []
+                for t in range(3):
+                    for g in range(BLK // LANES):
+                        cols = slice(g * LANES, (g + 1) * LANES)
+                        es.append(scores[t, rows, cols] * qvec[t, :, cols])
+                lane_sum[rows, :] = tree(jnp.add, es)
+            return carry
+
+        lax.fori_loop(0, BLK // (2 * ROWS), step, 0)
+        return to_row()
+
+    def scaled_col_sums(t):
+        groups = BLK // LANES
+
+        def step(i, sums):
+            rows = pl.ds(pl.multiple_of(i * STRIP, STRIP), STRIP)
+            a = bcast[rows, :]
+            out = []
+            for g in range(groups):
+                x = scores[t, rows, g * LANES:(g + 1) * LANES] * a
+                out.append(sums[g] + jnp.sum(x.reshape(STRIP // 8, 8, LANES), axis=0))
+            return tuple(out)
+
+        sums = lax.fori_loop(
+            0, BLK // STRIP, step,
+            tuple(jnp.zeros((8, LANES), jnp.float32) for _ in range(groups)),
+        )
+        return jnp.concatenate([jnp.sum(x, axis=0, keepdims=True) for x in sums], axis=1)
+
     def spread(v):
         for g in range(BLK // LANES):
             part = jnp.broadcast_to(v[:, g * LANES:(g + 1) * LANES], (LANES, LANES))
@@ -244,8 +316,7 @@
             copies[-1].start()
         for cp in copies:
             cp.wait()
-        top, e = lse2([row_box[it, j] for j in range(4)])
-        return top + log2((e[0] + e[1]) + (e[2] + e[3]))
+        return [row_box[it, j] for j in range(4)]
 
     def matches(d, block):
         b, live = extra_of(d)
@@ -256,9 +327,12 @@
         top, e = lse2(terms)
         return top + log2(functools.reduce(jnp.add, e))
 
-    def col_round(it):
+    def merge_sums(first, others):
+        return functools.reduce(jnp.add, [first] + [jnp.where(flag, x, 0.0) for flag, x in others])
+
+    def col_round(it, one_pass, merge):
         for t in range(3):
-            col_box[it, 0, t] = col_pass(t)
+            col_box[it, 0, t] = one_pass(t)
         copies = []
         for k in range(2):
             copies.append(pltpu.make_async_remote_copy(
@@ -277,12 +351,13 @@
         for cp in copies:
             cp.wait()
         before, after = col_box[it, 1, 2], col_box[it, 2, 2]
-        for b in range(2):
-            total = merge(
+        totals = [
+            merge(
                 col_box[it, 0, b],
                 [(matches(-1, base + b), before), (matches(1, base + b), after)],
             )
-            bvec[b] = ltgt - total
+            for b in range(2)
+        ]
         owner = jnp.where(
             from_before,
             jnp.where(my_pos == 0, col_box[it, 1, 0], col_box[it, 1, 1]),
@@ -294,8 +369,7 @@
             jnp.where(matches(2, my_block), 1, 0),
         ) == 1
         third = jnp.where(from_before, far_box[it, 0], far_box[it, 1])
-        total = merge(owner, [(my_live, col_box[it, 0, 2]), (third_flag, third)])
-        bvec[2] = jnp.where(my_live, ltgt - total, dead)
+        return totals + [merge(owner, [(my_live, col_box[it, 0, 2]), (third_flag, third)])]
 
     own_lse[...] = row_pass([0, 1], [None, None])
 
@@ -303,15 +377,26 @@
 
     extra_lse = jnp.where(my_live, row_pass([2], [None]), dead)
     top, e = lse2([own_lse[...], extra_lse])
-    total = row_round(0, top + log2(e[0] + e[1]))
-    for it in range(ITERS):
-        spread(lsrc - total)
-        col_round(it)
-        total = row_round(it + 1, row_pass([0, 1, 2], [bvec[0], bvec[1], bvec[2]]))
-    fpot_ref[...] = (epsilon * LN2) * (lsrc - total)
+    top, e = lse2(row_round(0, top + log2(e[0] + e[1])))
+    first_lse = top + log2((e[0] + e[1]) + (e[2] + e[3]))
+    spread(lsrc - first_lse)
+    totals = col_round(0, col_pass, merge)
     for b in range(2):
-        gpot_ref[b] = (epsilon * LN2) * bvec[b]
-    spread(total)
+        bvec[b] = ltgt - totals[b]
+    bvec[2] = jnp.where(my_live, ltgt - totals[2], dead)
+
+    e = row_round(1, plan_pass())
+    spread(1.0 / ((e[0] + e[1]) + (e[2] + e[3])))
+    totals = col_round(1, scaled_col_sums, merge_sums)
+    gap = ltgt - lsrc
+    for b in range(2):
+        qvec[b] = 1.0 / totals[b]
+        gpot_ref[b] = (epsilon * LN2) * (gap + bvec[b] - log2(totals[b]))
+    qvec[2] = jnp.where(my_live, 1.0 / totals[2], 0.0)
+    e = row_round(2, scaled_row_sums())
+    total = (e[0] + e[1]) + (e[2] + e[3])
+    fpot_ref[...] = (epsilon * LN2) * (lsrc - (first_lse + 2.0 * gap + log2(total)))
+    spread(1.0 / total)
 
     def bary(r0):
         rows = pl.ds(pl.multiple_of(r0, PIECE), PIECE)
@@ -319,7 +404,7 @@
         level = jnp.concatenate([level] * (BLK // LANES), axis=1)
         numer = None
         for t in range(3):
-            weights = jnp.exp2(scores[t, rows, :] + bvec[t] - level).astype(jnp.bfloat16)
+            weights = (scores[t, rows, :] * qvec[t] * level).astype(jnp.bfloat16)
             block = extra[...] if t == 2 else tgt_ref[t * BLK:(t + 1) * BLK, :]
             term = jnp.dot(weights, block, preferred_element_type=jnp.float32)
             numer = term if numer is None else numer + term
@@ -392,7 +477,7 @@
     wide_count = lax.axis_size("wide")
     narrow_count = lax.axis_size("narrow")
     group_blocks = tgt_blocks * narrow_count
-    assert src_blocks == 1 and tgt_blocks == 2 and narrow_count == 4
+    assert ITERS == 2 and src_blocks == 1 and tgt_blocks == 2 and narrow_count == 4
     assert pair_target.shape[1] == group_blocks + narrow_count and wide_count >= 5 and wide_count % 2 == 0
     scale = LOG2E / (math.sqrt(features) * epsilon)
     lsrc = -math.log2(wide_count * src_blocks * BLK)
@@ -400,6 +485,7 @@
     consts = (scale, lsrc, ltgt, group_blocks, tgt_blocks)
     vm = pl.BlockSpec(memory_space=pltpu.VMEM)
     sm = pl.BlockSpec(memory_space=pltpu.SMEM)
+    hbm = pl.BlockSpec(memory_space=pl.ANY)
     f32, bf16 = jnp.float32, jnp.bfloat16
     rounds = ITERS + 1
     dma = pltpu.SemaphoreType.DMA
@@ -410,9 +496,11 @@
             jax.ShapeDtypeStruct((tgt_blocks, 1, BLK), f32),
             jax.ShapeDtypeStruct((BLK, features), bf16),
         ),
-        in_specs=[sm, sm, vm, vm],
+        in_specs=[sm, sm, hbm, hbm],
         out_specs=(vm, vm, vm),
         scratch_shapes=[
+            pltpu.VMEM((src_blocks * BLK, features), bf16),
+            pltpu.VMEM((tgt_blocks * BLK, features), bf16),
             pltpu.VMEM((3, BLK, BLK), f32),
             pltpu.VMEM((BLK, features), bf16),
             pltpu.VMEM((BLK, features), bf16),
@@ -422,6 +510,7 @@
             pltpu.VMEM((BLK, LANES), f32),
             pltpu.VMEM((BLK, LANES), f32),
             pltpu.VMEM((1, BLK), f32),
+            pltpu.VMEM((3, 1, BLK), f32),
             pltpu.VMEM((1, BLK), f32),
             pltpu.VMEM((rounds, 4, 1, BLK), f32),
             pltpu.VMEM((ITERS, 3, 3, 1, BLK), f32),
@@ -439,6 +528,7 @@
             dma((NPIECE,)), dma((NPIECE,)),
             dma((NPIECE,)), dma((NPIECE,)),
             dma((NPIECE,)), dma((NPIECE,)),
+            dma((2,)),
         ],
         compiler_params=pltpu.CompilerParams(
             collective_id=0, has_side_effects=True, vmem_limit_bytes=48 * 1024 * 1024

time: 115 us -> 104 us (0.904)
  Pallas kernels: 109 us -> 98.5 us
    pallas_call x1, Pallas kernels: 109 us -> 98.5 us  [shards(): pl.pallas_call(functools.partial(kernel, wide_count, narrow_count, consts...]
where the time goes in v3:
time: 104 us
  Pallas kernels  98.5 us (95%)
  local copies, waits for them, and re-layouts  5.08 us (5%)
    pallas_call x1, Pallas kernels, shards(): pl.pallas_call(functools.partial(kernel, wide_count, narrow_count, consts...  98.5 us
    unnamed x9, local copies, waits for them, and re-layouts  5.08 us

profile of v3, /device:TPU:0, one launch (start us, length us, event | category | flops | bytes accessed | tf_op | source)
XLA Modules:
  0.0 104.3 jit_solution(6113283461925207973)
XLA Ops:
  0.6 0.0 copy-start
  0.6 1.4 %copy-done = bf16[1024,768]{1,0:T(8,128)(2,1)S(1)} copy-done((bf16[1024,768]{1,0:T(8,128)(2,1)S(1)}, bf16[1024,768]{1,0:T(8,128)(2,1)}, u32[]{:S(2)}) %copy-start) | copy-done | bytes 1572888
  2.0 0.0 copy-start.1
  2.0 0.7 copy-done.1
  2.7 0.0 copy-start.2
  2.7 0.7 copy-done.2
  3.4 98.5 %shard_map.67 = (f32[1,1024]{1,0:T(1,128)S(1)}, f32[2,1,1024]{2,1,0:T(1,128)S(1)}, bf16[1024,768]{1,0:T(8,128)(2,1)S(1)}) custom-call(s32[8,12]{1,0:T(8,128)S(1)} %copy-done.1, s32[8]{0:T(128)S(1)} %copy-done.2, bf16[1024,768]{1,0:T(8,128)(2,1)S(1)} %copy-done, bf16[2048,768]{1,0:T(8,128)(2,1)} %tgt_hbm.1), custom_call_target="tpu_custom_call" | custom-call | flops 9663676416 | bytes 6291456 | tf_op jit(solution)/shard_map/pallas_call | solution.py:492
  101.9 0.6 copy.10
  102.5 0.6 copy.11
  103.1 1.1 %copy.12 = bf16[1024,768]{1,0:T(8,128)(2,1)} copy(bf16[1024,768]{1,0:T(8,128)(2,1)S(1)} %get-tuple-element.14) | data formatting | bytes 3145728
Async XLA Ops:
  0.6 1.4 %copy-start = (bf16[1024,768]{1,0:T(8,128)(2,1)S(1)}, bf16[1024,768]{1,0:T(8,128)(2,1)}, u32[]{:S(2)}) copy-start(bf16[1024,768]{1,0:T(8,128)(2,1)} %src_hbm.1) | copy-start | bytes 4718596
  2.0 0.7 copy-start.1
  2.7 0.7 copy-start.2

commit v4 on v3

--- a/solution.py
+++ b/solution.py
@@ -393,18 +393,12 @@
         qvec[b] = 1.0 / totals[b]
         gpot_ref[b] = (epsilon * LN2) * (gap + bvec[b] - log2(totals[b]))
     qvec[2] = jnp.where(my_live, 1.0 / totals[2], 0.0)
-    e = row_round(2, scaled_row_sums())
-    total = (e[0] + e[1]) + (e[2] + e[3])
-    fpot_ref[...] = (epsilon * LN2) * (lsrc - (first_lse + 2.0 * gap + log2(total)))
-    spread(1.0 / total)
 
     def bary(r0):
         rows = pl.ds(pl.multiple_of(r0, PIECE), PIECE)
-        level = bcast[rows, :]
-        level = jnp.concatenate([level] * (BLK // LANES), axis=1)
         numer = None
         for t in range(3):
-            weights = (scores[t, rows, :] * qvec[t] * level).astype(jnp.bfloat16)
+            weights = (scores[t, rows, :] * qvec[t]).astype(jnp.bfloat16)
             block = extra[...] if t == 2 else tgt_ref[t * BLK:(t + 1) * BLK, :]
             term = jnp.dot(weights, block, preferred_element_type=jnp.float32)
             numer = term if numer is None else numer + term
@@ -451,13 +445,19 @@
 
     lax.fori_loop(0, NPIECE, send_part, 0)
 
+    e = row_round(2, scaled_row_sums())
+    total = (e[0] + e[1]) + (e[2] + e[3])
+    fpot_ref[...] = (epsilon * LN2) * (lsrc - (first_lse + 2.0 * gap + log2(total)))
+    spread(1.0 / total)
+
     def finish(p, carry):
         cross_copy(p).wait()
         both = cross_out[piece_rows(p), :].astype(jnp.float32) + cross_in[
             piece_rows(p), :
         ].astype(jnp.float32)
         rows = pl.ds(pl.multiple_of(mine0 + p * PIECE, PIECE), PIECE)
-        map_ref[rows, :] = both.astype(jnp.bfloat16)
+        level = jnp.concatenate([bcast[rows, :]] * (both.shape[1] // LANES), axis=1)
+        map_ref[rows, :] = (both * level).astype(jnp.bfloat16)
         final_copy(p).start()
         return carry
 

time: 104 us -> 102 us (0.981)
  Pallas kernels: 98.5 us -> 96 us
    pallas_call x1, Pallas kernels: 98.5 us -> 96 us  [shards(): pl.pallas_call(functools.partial(kernel, wide_count, narrow_count, consts...]
where the time goes in v4:
time: 102 us
  Pallas kernels  96 us (94%)
  local copies, waits for them, and re-layouts  5.08 us (5%)
    pallas_call x1, Pallas kernels, shards(): pl.pallas_call(functools.partial(kernel, wide_count, narrow_count, consts...  96 us
    unnamed x9, local copies, waits for them, and re-layouts  5.08 us

profile of v4, /device:TPU:0, one launch (start us, length us, event | category | flops | bytes accessed | tf_op | source)
XLA Modules:
  0.0 101.7 jit_solution(977441582794293301)
XLA Ops:
  0.6 0.0 copy-start
  0.6 1.4 %copy-done = bf16[1024,768]{1,0:T(8,128)(2,1)S(1)} copy-done((bf16[1024,768]{1,0:T(8,128)(2,1)S(1)}, bf16[1024,768]{1,0:T(8,128)(2,1)}, u32[]{:S(2)}) %copy-start) | copy-done | bytes 1572888
  2.0 0.0 copy-start.1
  2.0 0.7 copy-done.1
  2.7 0.0 copy-start.2
  2.7 0.7 copy-done.2
  3.4 96.0 %shard_map.67 = (f32[1,1024]{1,0:T(1,128)S(1)}, f32[2,1,1024]{2,1,0:T(1,128)S(1)}, bf16[1024,768]{1,0:T(8,128)(2,1)S(1)}) custom-call(s32[8,12]{1,0:T(8,128)S(1)} %copy-done.1, s32[8]{0:T(128)S(1)} %copy-done.2, bf16[1024,768]{1,0:T(8,128)(2,1)S(1)} %copy-done, bf16[2048,768]{1,0:T(8,128)(2,1)} %tgt_hbm.1), custom_call_target="tpu_custom_call" | custom-call | flops 9663676416 | bytes 6291456 | tf_op jit(solution)/shard_map/pallas_call | solution.py:492
  99.4 0.6 copy.10
  100.0 0.6 copy.11
  100.6 1.1 %copy.12 = bf16[1024,768]{1,0:T(8,128)(2,1)} copy(bf16[1024,768]{1,0:T(8,128)(2,1)S(1)} %get-tuple-element.14) | data formatting | bytes 3145728
Async XLA Ops:
  0.6 1.4 %copy-start = (bf16[1024,768]{1,0:T(8,128)(2,1)S(1)}, bf16[1024,768]{1,0:T(8,128)(2,1)}, u32[]{:S(2)}) copy-start(bf16[1024,768]{1,0:T(8,128)(2,1)} %src_hbm.1) | copy-start | bytes 4718596
  2.0 0.7 copy-start.1
  2.7 0.7 copy-start.2
